TPU v7x, 32 devices: a whole 2x2x4 slice. The times are simulated.
32 devices in a mesh: runs: 2 (over y), tiles: 16 (over z, x, core).
Axes of the slice: x: 2, y: 2, z: 4, core: 2. Of those that a mesh axis runs over, the one named last changes fastest.
Arguments:
- features: bfloat16 [32, 256, 2048], P(('runs', 'tiles')), parts along dimension 0, may hold values from -6 to 6
- conv_weight: bfloat16 [2, 2, 9, 256, 256], replicated, may hold values from -0.125 to 0.125
- proj_weight: bfloat16 [2, 256, 128], replicated, may hold values from -0.375 to 0.375
- back_weight: bfloat16 [2, 128, 256], replicated, may hold values from -0.5 to 0.5
- sea_fraction: float32 [16, 2048], P('tiles'), may hold values from 0 to 1
- halo_source: int32 [16, 2, 128], P('tiles'), may hold values from 0 to 256, as said below
- src_cells: int32 [16, 5, 4, 128], P('tiles'), may hold values from 0 to 2047
- dst_cells: int32 [16, 5, 4, 128], P('tiles'), may hold values from 0 to 2048, as said below
Outputs:
- updated: bfloat16 [32, 256, 2048], P(('runs', 'tiles')), parts along dimension 0
There are 2 independent parts, one for each index of `runs`. A program takes and returns all parts, laid end to end along the dimension named above; an argument that names none is the same for every part. Nothing has to cross between parts.
Inputs may be any that keep to these rules, and one draw needn't show every extreme that they name: `halo_source`: the value 2 * 128 means a zero halo cell and occurs on the lower side of the ocean tile of local index 0; the atmosphere tiles at both ends of their arc and the last ocean tile read their own edge row on their outer side. `dst_cells`: entry 2048 marks an unused block; a block is used only if its source tile lies in the other component, and every tile uses all 4 blocks of offset 0.
All inputs are finite; a program needn't handle non-finite values.
Results may differ from a plain program's by a relative error of at most 0.0085.
Values may be sent and summed in bfloat16 or wider, within the bound.
A program may use at most 64 MiB of HBM per device.

v0:
```python
import jax
import jax.numpy as jnp
from jax import lax
from jax.sharding import PartitionSpec as P


def with_halo(x, sides, width):
    for axis, dim in sides:
        peers, length = (lax.axis_size(axis), x.shape[dim])
        up = [(i, (i + 1) % peers) for i in range(peers)]
        down = [(j, i) for i, j in up]
        last = lax.slice_in_dim(x, length - width, length, axis=dim)
        first = lax.slice_in_dim(x, 0, width, axis=dim)
        before = lax.ppermute(last, axis, up)
        after = lax.ppermute(first, axis, down)
        x = jnp.concatenate([before, x, after], axis=dim)
    return x


def passed_along(value, axis, steps):
    count = lax.axis_size(axis)
    pairs = [(source, (source + steps) % count) for source in range(count)]
    return lax.ppermute(value, axis, pairs)


def residual_block(state, kernel, wet_weight, halo_table):
    channels, cell_count = state.shape
    row_cells = halo_table.shape[1]
    lat_rows = cell_count // row_cells
    activated = jax.nn.gelu(state.astype(jnp.float32), approximate=True).astype(jnp.bfloat16)
    activated = activated.reshape(channels, lat_rows, row_cells)
    boundary = jnp.stack([activated[:, 0, :], activated[:, lat_rows - 1, :]])
    extended = with_halo(boundary, (("tiles", 0),), 1)
    zero_col = jnp.zeros((channels, 1), jnp.bfloat16)
    lower_src = jnp.concatenate([extended[0], activated[:, 0, :], zero_col], axis=1)
    upper_src = jnp.concatenate([extended[3], activated[:, lat_rows - 1, :], zero_col], axis=1)
    lower_row = jnp.take(lower_src, halo_table[0], axis=1)
    upper_row = jnp.take(upper_src, halo_table[1], axis=1)
    padded = jnp.concatenate([lower_row[:, None], activated, upper_row[:, None]], axis=1)
    convolved = jnp.zeros((channels, lat_rows, row_cells), jnp.float32)
    for row_off in range(3):
        for col_off in range(3):
            shifted = jnp.roll(padded[:, row_off : row_off + lat_rows, :], 1 - col_off, axis=2)
            convolved = convolved + jnp.einsum(
                "io,irc->orc",
                kernel[row_off * 3 + col_off],
                shifted,
                preferred_element_type=jnp.float32,
            )
    return (
        state.astype(jnp.float32) + wet_weight[None, :] * convolved.reshape(channels, cell_count)
    ).astype(jnp.bfloat16)


def remap_add(state, project_weight, return_weight, source_table, target_table, half_count):
    channels, cell_count = state.shape
    offset_count = source_table.shape[0]
    reach_slots = offset_count // 2
    projected = jnp.einsum(
        "cn,ck->nk", state, project_weight, preferred_element_type=jnp.float32
    ).astype(jnp.bfloat16)
    outgoing = projected[source_table]
    incoming = []
    for offset_slot in range(offset_count):
        incoming.append(
            passed_along(outgoing[offset_slot], "tiles", half_count + offset_slot - reach_slots)
        )
    received = jnp.stack(incoming)
    coupling = received.shape[-1]
    summed = jnp.zeros((cell_count, coupling), jnp.float32)
    summed = summed.at[target_table.reshape(-1)].add(
        received.reshape(-1, coupling).astype(jnp.float32), mode="drop"
    )
    remapped = summed.astype(jnp.bfloat16)
    returned = jnp.einsum("nk,ko->on", remapped, return_weight, preferred_element_type=jnp.float32)
    return (state.astype(jnp.float32) + returned).astype(jnp.bfloat16)


def on_device(
    features, conv_weight, proj_weight, back_weight, sea_fraction, halo_source, src_cells, dst_cells
):
    tile_total = lax.axis_size("tiles")
    half_count = tile_total // 2
    position = (lax.axis_index("tiles") + half_count // 2) % tile_total
    component = (position >= half_count).astype(jnp.int32)
    wet_weight = jnp.where(component == 1, sea_fraction[0], jnp.float32(1.0))
    kernels = lax.dynamic_index_in_dim(conv_weight, component, 0, keepdims=False)
    project_weight = lax.dynamic_index_in_dim(proj_weight, component, 0, keepdims=False)
    return_weight = lax.dynamic_index_in_dim(back_weight, component, 0, keepdims=False)
    state = features[0]
    state = residual_block(state, kernels[0], wet_weight, halo_source[0])
    state = remap_add(state, project_weight, return_weight, src_cells[0], dst_cells[0], half_count)
    state = residual_block(state, kernels[1], wet_weight, halo_source[0])
    return state[None]


def solution(mesh):
    placed = (
        P(("runs", "tiles"), None, None),
        P(),
        P(),
        P(),
        P("tiles", None),
        P("tiles", None, None),
        P("tiles", None, None, None),
        P("tiles", None, None, None),
    )
    return jax.shard_map(
        on_device,
        mesh=mesh,
        in_specs=placed,
        out_specs=P(("runs", "tiles"), None, None),
        check_vma=False,
    )
```

profile of v0, /device:TPU:0, one launch (start us, length us, event | category | flops | bytes accessed | tf_op | source)
XLA Modules:
  0.0 132.3 jit_solution(9170165621772137968)
XLA Ops:
  0.0 1.5 %copy.9 = f32[1,256,2048]{1,2,0:T(8,128)S(1)} copy(bf16[1,256,2048]{2,1,0:T(8,128)(2,1)} %param.10) | data formatting | bytes 3145728 | tf_op jit(solution)/shard_map/convert_element_type | solution.py:51
  1.6 0.7 fusion.8
  2.7 5.0 %collective-permute-start.1 = (bf16[1,256,128]{1,2,0:T(8,128)(2,1)S(1)}, bf16[1,256,128]{1,2,0:T(8,128)(2,1)S(1)}, u32[]{:S(2)}, u32[]{:S(2)}) collective-permute-start(bf16[1,256,128]{1,2,0:T(8,128)(2,1)S(1)} %get-tuple-element.52), channel_id=1, source_target_pairs={{1,0},{2,1},{3,2},{4,3},{5,4},{6,5},{7,6},{8,7},{9,8},{10,9},{11,1... | collective-permute-start | bytes 196616 | tf_op jit(solution)/shard_map/ppermute | solution.py:15
  8.0 3.6 %fusion.43 = f32[256,2048]{0,1} fusion(bf16[1,256,2048]{2,1,0:T(8,128)(2,1)} %param.10, bf16[2,2,9,256,256]{4,3,2,1,0:T(8,128)(2,1)} %param.11, s32[]{:T(128)S(6)} %select_n.54, s32[]{:T(128)S(6)} %add.180), kind=kOutput, calls=%fused_computation.76 | convolution fusion | flops 273678336 | bytes 3276808
  11.8 0.8 gather_fusion.1
  12.7 0.8 gather_fusion.2
  13.7 1.4 %fusion.37 = (bf16[256,16,127]{0,2,1:T(8,128)(2,1)S(1)}, bf16[256,16,127]{0,2,1:T(8,128)(2,1)S(1)}, bf16[256,16,127]{0,2,1:T(8,128)(2,1)S(1)}, bf16[256,16,127]{...) fusion(bf16[256,1,128]{0,2,1:T(8,128)(2,1)S(1)} %select_bitcast_fusion.3, ...), kind=kLoop, calls=%fused_computation.71 | loop fusion | flops 2080768 | bytes 9519104 | tf_op jit(solution)/shard_map/concatenate | solution.py:39
  15.1 1.9 %fusion.38 = (bf16[256,16,128]{0,2,1:T(8,128)(2,1)S(1)}, bf16[256,16,128]{0,2,1:T(8,128)(2,1)S(1)}, bf16[256,16,128]{0,2,1:T(8,128)(2,1)S(1)}, bf16[256,16,128]{...) fusion(bf16[256,1,128]{0,2,1:T(8,128)(2,1)S(1)} %select_bitcast_fusion.3, ...), kind=kLoop, calls=%fused_computation.72 | loop fusion | flops 16777216 | bytes 11632640 | tf_op jit(solution)/shard_map/concatenate | solution.py:39
  16.9 2.7 %fusion.76 = f32[256,2048]{0,1} fusion(bf16[256,2048]{0,1:T(8,128)(2,1)S(1)} %bitcast.240, bf16[2,2,9,256,256]{4,3,2,1,0:T(8,128)(2,1)} %param.11, s32[]{:T(128)S(6)} %select_n.54), kind=kOutput, calls=%fused_computation.142 | convolution fusion | flops 268435456 | bytes 3276804
  20.2 1.3 %fusion.73 = f32[256,2048]{0,1:S(1)} fusion(bf16[256,2048]{0,1:T(8,128)(2,1)S(1)} %bitcast.245, bf16[2,2,9,256,256]{4,3,2,1,0:T(8,128)(2,1)} %param.11, s32[]{:T(128)S(6)} %select_n.54, s32[]{:T(128)S(6)} %add.179), kind=kOutput, calls=%fused_computation.136 | convolution fusion | flops 268435456 | bytes 3276808
  21.5 1.3 %fusion.69 = f32[256,2048]{0,1:S(1)} fusion(bf16[256,2048]{0,1:T(8,128)(2,1)S(1)} %bitcast.234, bf16[2,2,9,256,256]{4,3,2,1,0:T(8,128)(2,1)} %param.11, s32[]{:T(128)S(6)} %select_n.54, s32[]{:T(128)S(6)} %add.184), kind=kOutput, calls=%fused_computation.127 | convolution fusion | flops 268435456 | bytes 3276808
  22.8 1.3 %fusion.70 = f32[256,2048]{0,1:S(1)} fusion(bf16[256,2048]{0,1:T(8,128)(2,1)S(1)} %bitcast.233, bf16[2,2,9,256,256]{4,3,2,1,0:T(8,128)(2,1)} %param.11, s32[]{:T(128)S(6)} %select_n.54, s32[]{:T(128)S(6)} %add.183), kind=kOutput, calls=%fused_computation.129 | convolution fusion | flops 268435456 | bytes 3276808
  24.2 1.3 %fusion.71 = f32[256,2048]{0,1:S(1)} fusion(bf16[256,2048]{0,1:T(8,128)(2,1)S(1)} %bitcast.232, bf16[2,2,9,256,256]{4,3,2,1,0:T(8,128)(2,1)} %param.11, s32[]{:T(128)S(6)} %select_n.54, s32[]{:T(128)S(6)} %add.182), kind=kOutput, calls=%fused_computation.131 | convolution fusion | flops 268435456 | bytes 3276808
  25.5 1.3 %fusion.74 = f32[256,2048]{0,1:S(1)} fusion(bf16[256,2048]{0,1:T(8,128)(2,1)S(1)} %bitcast.231, bf16[2,2,9,256,256]{4,3,2,1,0:T(8,128)(2,1)} %param.11, s32[]{:T(128)S(6)} %select_n.54, s32[]{:T(128)S(6)} %add.178), kind=kOutput, calls=%fused_computation.138 | convolution fusion | flops 268435456 | bytes 3276808
  26.9 2.7 %fusion.72 = f32[256,2048]{0,1} fusion(bf16[256,2048]{0,1:T(8,128)(2,1)S(1)} %bitcast.242, bf16[2,2,9,256,256]{4,3,2,1,0:T(8,128)(2,1)} %param.11, s32[]{:T(128)S(6)} %select_n.54, s32[]{:T(128)S(6)} %add.181), kind=kOutput, calls=%fused_computation.133 | convolution fusion | flops 268435456 | bytes 3276808
  29.5 2.7 %fusion.75 = f32[256,2048]{0,1} fusion(bf16[256,2048]{0,1:T(8,128)(2,1)S(1)} %bitcast.230, bf16[2,2,9,256,256]{4,3,2,1,0:T(8,128)(2,1)} %param.11, s32[]{:T(128)S(6)} %select_n.54, s32[]{:T(128)S(6)} %add.177), kind=kOutput, calls=%fused_computation.140 | convolution fusion | flops 268435456 | bytes 3276808
  32.3 5.3 %add_add_fusion.1 = f32[256,16,128]{0,2,1:T(8,128)S(1)} fusion(f32[256,16,128]{0,2,1:T(8,128)S(1)} %bitcast.219, f32[256,16,128]{0,2,1:T(8,128)S(1)} %bitcast.221, f32[256,16,128]{0,2,1:T(8,128)S(1)} %bitcast.222, f32[256,16,128]{0,2,1:T(8,128)} %bitcast.225, f32[256,16,128]{0,2,1:T(8,128)} %bitcast.247, f32[256,16,128]{0,2,1:T(8,128)S(1)} %bitcast.218, ...), kind=kLoop, calls=%fused_computation.46 | loop fusion | flops 4194304 | bytes 20971520 | tf_op jit(solution)/shard_map/add | solution.py:44
  37.5 1.8 %copy.12 = f32[1,256,2048]{2,1,0:T(8,128)} copy(f32[1,256,2048]{1,2,0:T(8,128)S(1)} %bitcast.210) | data formatting | bytes 4194304 | tf_op jit(solution)/shard_map/reshape | solution.py:51
  39.4 2.4 %convolution_convert_fusion = bf16[2048,128]{1,0:T(8,128)(2,1)S(1)} fusion(f32[1,256,2048]{2,1,0:T(8,128)} %copy.12, bf16[1,256,2048]{2,1,0:T(8,128)(2,1)} %param.10, f32[2048]{0:T(1024)S(1)} %bitcast.251, bf16[2,256,128]{2,1,0:T(8,128)(2,1)S(1)} %copy-done.5, s32[]{:T(128)S(6)} %select_n.54), kind=kOutput, calls=%fused_computation.20 | convolution fusion | flops 136577024 | bytes 3743748 | tf_op jit(solution)/shard_map/cn,ck->nk/dot_general | solution.py:59
  41.8 5.1 %gather_fusion = bf16[2560,128]{1,0:T(8,128)(2,1)S(1)} fusion(bf16[2048,128]{1,0:T(8,128)(2,1)S(1)} %convolution_convert_fusion, s32[3072]{0:T(1024)S(1)} %pad_clamp_fusion), kind=kCustom, calls=%fused_computation.4 | custom fusion | bytes 1320960 | tf_op jit(solution)/shard_map/gather | solution.py:62
  46.9 0.8 fusion.109
  47.9 1.3 %fusion.81 = s32[2560]{0:T(1024)} fusion(s32[2560,1]{0,1:T(1,128)} %bitcast.258), kind=kLoop, calls=%fused_computation.168 | loop fusion | flops 7680 | bytes 20480 | tf_op jit(solution)/shard_map/select_n | solution.py:71
  49.2 1.8 %copy.11 = f32[256,2048]{1,0:T(8,128)} copy(f32[256,2048]{0,1:T(8,128)S(1)} %bitcast.211) | data formatting | bytes 4194304 | tf_op jit(solution)/shard_map/reshape | solution.py:51
  51.0 2.6 %collective-permute-start.5 = (bf16[4,128,128]{2,1,0:T(8,128)(2,1)}, bf16[4,128,128]{2,1,0:T(8,128)(2,1)S(1)}, u32[]{:S(2)}, u32[]{:S(2)}) collective-permute-start(bf16[4,128,128]{2,1,0:T(8,128)(2,1)} %bitcast.56), channel_id=1, source_target_pairs={{0,9},{1,10},{2,11},{3,12},{4,13},{5,14},{6,15},{7,0},{8,1},{9,2},... | collective-permute-start | bytes 393224 | tf_op jit(solution)/shard_map/ppermute | solution.py:23
  53.6 1.1 collective-permute-start.6
  54.7 1.2 collective-permute-start.4
  55.9 2.1 %collective-permute-start.3 = (bf16[4,128,128]{2,1,0:T(8,128)(2,1)}, bf16[4,128,128]{2,1,0:T(8,128)(2,1)S(1)}, u32[]{:S(2)}, u32[]{:S(2)}) collective-permute-start(bf16[4,128,128]{2,1,0:T(8,128)(2,1)} %bitcast.52), channel_id=1, source_target_pairs={{0,7},{1,8},{2,9},{3,10},{4,11},{5,12},{6,13},{7,14},{8,15},{9,0},... | collective-permute-start | bytes 393224 | tf_op jit(solution)/shard_map/ppermute | solution.py:23
  57.9 18.8 %collective-permute-done.3 = bf16[4,128,128]{2,1,0:T(8,128)(2,1)S(1)} collective-permute-done((bf16[4,128,128]{2,1,0:T(8,128)(2,1)}, bf16[4,128,128]{2,1,0:T(8,128)(2,1)S(1)}, u32[]{:S(2)}, u32[]{:S(2)}) %collective-permute-start.3) | collective-permute-done | bytes 131104 | tf_op jit(solution)/shard_map/ppermute | solution.py:23
  76.9 14.6 %scatter_custom_fusion = f32[2048,128]{1,0:T(8,128)S(1)} fusion(s32[2560]{0:T(1024)} %fusion.81, bf16[2560,128]{1,0:T(8,128)(2,1)S(1)} %bitcast.248, f32[]{:T(128)} %constant.62.clone.1), kind=kCustom, calls=%fused_computation.59 | custom fusion | flops 655360 | bytes 1704448 | tf_op jit(solution)/shard_map/scatter-add | solution.py:71
  91.5 3.7 %fusion.23 = (bf16[256,2048]{1,0:T(8,128)(2,1)S(1)}, bf16[256,2048]{1,0:T(8,128)(2,1)}) fusion(f32[2048,128]{1,0:T(8,128)S(1)} %scatter_custom_fusion, bf16[2,128,256]{2,1,0:T(8,128)(2,1)S(1)} %copy-done, s32[]{:T(128)S(6)} %select_n.54, f32[256,2048]{1,0:T(8,128)} %copy.11, f32[2048]{0:T(1024)S(1)} %bitcast.252, bf16[1,256,2048]{2,1,0:T(8,128)(2,1)S(1)} %copy-done.2), kind=kOutput, calls=%fused_computation.43 | convolution fusion | flops 143392768 | bytes 6365188 | tf_op jit(solution)/shard_map/nk,ko->on/dot_general | solution.py:75
  95.2 0.5 copy.25
  95.8 4.4 %collective-permute-start.8 = (bf16[1,256,128]{1,2,0:T(8,128)(2,1)S(1)}, bf16[1,256,128]{1,2,0:T(8,128)(2,1)S(1)}, u32[]{:S(2)}, u32[]{:S(2)}) collective-permute-start(bf16[1,256,128]{1,2,0:T(8,128)(2,1)S(1)} %get-tuple-element.39), channel_id=1, source_target_pairs={{1,0},{2,1},{3,2},{4,3},{5,4},{6,5},{7,6},{8,7},{9,8},{10,9},{11,1... | collective-permute-start | bytes 196616 | tf_op jit(solution)/shard_map/ppermute | solution.py:15
  100.3 3.3 %fusion.64 = f32[256,2048]{0,1} fusion(bf16[2,2,9,256,256]{4,3,2,1,0:T(8,128)(2,1)} %param.11, s32[]{:T(128)S(6)} %select_n.54, s32[]{:T(128)S(6)} %add.177, s32[]{:T(128)S(6)} %add.180, bf16[256,2048]{1,0:T(8,128)(2,1)S(1)} %copy-done.3), kind=kOutput, calls=%fused_computation.117 | convolution fusion | flops 273678336 | bytes 3276812
  103.7 0.8 gather_fusion.3
  104.6 1.0 gather_fusion.4
  105.7 1.4 %fusion.31 = (bf16[256,16,127]{0,2,1:T(8,128)(2,1)S(1)}, bf16[256,16,127]{0,2,1:T(8,128)(2,1)S(1)}, bf16[256,16,127]{0,2,1:T(8,128)(2,1)S(1)}, bf16[256,16,127]{...) fusion(bf16[256,1,128]{0,2,1:T(8,128)(2,1)S(1)} %get-tuple-element.70, ...), kind=kLoop, calls=%fused_computation.65 | loop fusion | flops 2080768 | bytes 9519104 | tf_op jit(solution)/shard_map/concatenate | solution.py:39
  107.5 1.3 %fusion.65 = f32[256,2048]{0,1:S(1)} fusion(bf16[256,2048]{0,1:T(8,128)(2,1)S(1)} %bitcast.243, bf16[2,2,9,256,256]{4,3,2,1,0:T(8,128)(2,1)} %param.11, s32[]{:T(128)S(6)} %select_n.54, s32[]{:T(128)S(6)} %add.177, s32[]{:T(128)S(6)} %add.179), kind=kOutput, calls=%fused_computation.119 | convolution fusion | flops 268435456 | bytes 3276812
  109.0 1.3 %fusion.63 = f32[256,2048]{0,1:S(1)} fusion(bf16[256,2048]{0,1:T(8,128)(2,1)S(1)} %bitcast.244, bf16[2,2,9,256,256]{4,3,2,1,0:T(8,128)(2,1)} %param.11, s32[]{:T(128)S(6)} %select_n.54, s32[]{:T(128)S(6)} %add.177, s32[]{:T(128)S(6)} %add.181), kind=kOutput, calls=%fused_computation.115 | convolution fusion | flops 268435456 | bytes 3276812
  110.3 1.9 %fusion.32 = (bf16[256,16,128]{0,2,1:T(8,128)(2,1)S(1)}, bf16[256,16,128]{0,2,1:T(8,128)(2,1)S(1)}, bf16[256,16,128]{0,2,1:T(8,128)(2,1)S(1)}, bf16[256,16,128]{...) fusion(bf16[256,1,128]{0,2,1:T(8,128)(2,1)S(1)} %get-tuple-element.70, ...), kind=kLoop, calls=%fused_computation.66 | loop fusion | flops 16777216 | bytes 11632640 | tf_op jit(solution)/shard_map/concatenate | solution.py:39
  112.2 1.3 %fusion.68 = f32[256,2048]{0,1:S(1)} fusion(bf16[256,2048]{0,1:T(8,128)(2,1)S(1)} %bitcast.241, bf16[2,2,9,256,256]{4,3,2,1,0:T(8,128)(2,1)} %param.11, s32[]{:T(128)S(6)} %select_n.54, s32[]{:T(128)S(6)} %add.177), kind=kOutput, calls=%fused_computation.125 | convolution fusion | flops 268435456 | bytes 3276808
  113.5 1.3 %fusion.67 = f32[256,2048]{0,1:S(1)} fusion(bf16[256,2048]{0,1:T(8,128)(2,1)S(1)} %bitcast.239, bf16[2,2,9,256,256]{4,3,2,1,0:T(8,128)(2,1)} %param.11, s32[]{:T(128)S(6)} %select_n.54, s32[]{:T(128)S(6)} %add.177), kind=kOutput, calls=%fused_computation.123 | convolution fusion | flops 268435456 | bytes 3276808
  114.9 1.3 %fusion.66 = f32[256,2048]{0,1:S(1)} fusion(bf16[256,2048]{0,1:T(8,128)(2,1)S(1)} %bitcast.238, bf16[2,2,9,256,256]{4,3,2,1,0:T(8,128)(2,1)} %param.11, s32[]{:T(128)S(6)} %select_n.54, s32[]{:T(128)S(6)} %add.177, s32[]{:T(128)S(6)} %add.178), kind=kOutput, calls=%fused_computation.121 | convolution fusion | flops 268435456 | bytes 3276812
  116.2 1.3 %fusion.60 = f32[256,2048]{0,1:S(1)} fusion(bf16[256,2048]{0,1:T(8,128)(2,1)S(1)} %bitcast.237, bf16[2,2,9,256,256]{4,3,2,1,0:T(8,128)(2,1)} %param.11, s32[]{:T(128)S(6)} %select_n.54, s32[]{:T(128)S(6)} %add.177, s32[]{:T(128)S(6)} %add.184), kind=kOutput, calls=%fused_computation.109 | convolution fusion | flops 268435456 | bytes 3276812
  117.5 2.7 %fusion.61 = f32[256,2048]{0,1} fusion(bf16[256,2048]{0,1:T(8,128)(2,1)S(1)} %bitcast.236, bf16[2,2,9,256,256]{4,3,2,1,0:T(8,128)(2,1)} %param.11, s32[]{:T(128)S(6)} %select_n.54, s32[]{:T(128)S(6)} %add.177, s32[]{:T(128)S(6)} %add.183), kind=kOutput, calls=%fused_computation.111 | convolution fusion | flops 268435456 | bytes 3276812
  120.2 2.7 %fusion.62 = f32[256,2048]{0,1} fusion(bf16[256,2048]{0,1:T(8,128)(2,1)S(1)} %bitcast.235, bf16[2,2,9,256,256]{4,3,2,1,0:T(8,128)(2,1)} %param.11, s32[]{:T(128)S(6)} %select_n.54, s32[]{:T(128)S(6)} %add.177, s32[]{:T(128)S(6)} %add.182), kind=kOutput, calls=%fused_computation.113 | convolution fusion | flops 268435456 | bytes 3276812
  122.9 6.0 %add_add_fusion = f32[256,16,128]{0,2,1:T(8,128)} fusion(f32[256,16,128]{0,2,1:T(8,128)S(1)} %bitcast.217, f32[256,16,128]{0,2,1:T(8,128)} %bitcast.220, f32[256,16,128]{0,2,1:T(8,128)} %bitcast.224, f32[256,16,128]{0,2,1:T(8,128)S(1)} %bitcast.213, f32[256,16,128]{0,2,1:T(8,128)} %bitcast.246, f32[256,16,128]{0,2,1:T(8,128)S(1)} %bitcast.212, ...), kind=kLoop, calls=%fused_computation.45 | loop fusion | flops 4194304 | bytes 20971520 | tf_op jit(solution)/shard_map/add | solution.py:44
  128.9 2.0 %copy.24 = f32[256,2048]{1,0:T(8,128)S(1)} copy(f32[256,2048]{0,1:T(8,128)} %bitcast.228) | data formatting | bytes 4194304 | tf_op jit(solution)/shard_map/reshape | solution.py:51
  131.0 1.3 fusion.39
  (65 shorter events, 2.6 us)
Async XLA Ops:
  0.0 91.5 %copy-start = (bf16[2,128,256]{2,1,0:T(8,128)(2,1)S(1)}, bf16[2,128,256]{2,1,0:T(8,128)(2,1)}, u32[]{:S(2)}) copy-start(bf16[2,128,256]{2,1,0:T(8,128)(2,1)} %param.13) | copy-start | bytes 393220
  1.5 6.3 %copy-start.13 = (s32[1,2,128]{2,1,0:T(2,128)S(1)}, s32[1,2,128]{2,1,0:T(2,128)}, u32[]{:S(2)}) copy-start(s32[1,2,128]{2,1,0:T(2,128)} %param.15) | copy-start | bytes 3076
  1.5 6.4 %copy-start.6 = (s32[1,5,4,128]{3,2,1,0:T(4,128)S(1)}, s32[1,5,4,128]{3,2,1,0:T(4,128)}, u32[]{:S(2)}) copy-start(s32[1,5,4,128]{3,2,1,0:T(4,128)} %param.16) | copy-start | bytes 30724
  1.5 6.4 %copy-start.7 = (f32[1,2048]{1,0:T(1,128)S(1)}, f32[1,2048]{1,0:T(1,128)}, u32[]{:S(2)}) copy-start(f32[1,2048]{1,0:T(1,128)} %param.14) | copy-start | bytes 24580
  2.2 9.4 %collective-permute-start = (bf16[1,256,128]{1,2,0:T(8,128)(2,1)S(1)}, bf16[1,256,128]{1,2,0:T(8,128)(2,1)S(1)}, u32[]{:S(2)}, u32[]{:S(2)}) collective-permute-start(bf16[1,256,128]{1,2,0:T(8,128)(2,1)S(1)} %get-tuple-element.50), channel_id=1, source_target_pairs={{0,1},{1,2},{2,3},{3,4},{4,5},{5,6},{6,7},{7,8},{8,9},{9,10},{10,1... | collective-permute-start | bytes 196616 | tf_op jit(solution)/shard_map/ppermute | solution.py:14
  2.7 8.9 %collective-permute-start.1 = (bf16[1,256,128]{1,2,0:T(8,128)(2,1)S(1)}, bf16[1,256,128]{1,2,0:T(8,128)(2,1)S(1)}, u32[]{:S(2)}, u32[]{:S(2)}) collective-permute-start(bf16[1,256,128]{1,2,0:T(8,128)(2,1)S(1)} %get-tuple-element.52), channel_id=1, source_target_pairs={{1,0},{2,1},{3,2},{4,3},{5,4},{6,5},{7,6},{8,7},{9,8},{10,9},{11,1... | collective-permute-start | bytes 196616 | tf_op jit(solution)/shard_map/ppermute | solution.py:15
  7.9 4.8 %copy-start.9 = (pred[128]{0:T(512)(128)(4,1)}, pred[128]{0:T(512)(128)(4,1)S(1)}, u32[]{:S(2)}) copy-start(pred[128]{0:T(512)(128)(4,1)S(1)} %get-tuple-element.6) | copy-start | bytes 388
  7.9 5.7 %copy-start.11 = (pred[128]{0:T(512)(128)(4,1)}, pred[128]{0:T(512)(128)(4,1)S(1)}, u32[]{:S(2)}) copy-start(pred[128]{0:T(512)(128)(4,1)S(1)} %get-tuple-element.63) | copy-start | bytes 388
  11.6 3.4 %copy-start.8 = (s32[1024]{0:T(1024)}, s32[1024]{0:T(1024)S(1)}, u32[]{:S(2)}) copy-start(s32[1024]{0:T(1024)S(1)} %pad_clamp_fusion.1) | copy-start | bytes 12292
  37.5 1.9 %copy-start.5 = (bf16[2,256,128]{2,1,0:T(8,128)(2,1)S(1)}, bf16[2,256,128]{2,1,0:T(8,128)(2,1)}, u32[]{:S(2)}) copy-start(bf16[2,256,128]{2,1,0:T(8,128)(2,1)} %param.12) | copy-start | bytes 393220
  47.6 10.3 %collective-permute-start.2 = (bf16[4,128,128]{2,1,0:T(8,128)(2,1)S(1)}, bf16[4,128,128]{2,1,0:T(8,128)(2,1)S(1)}, u32[]{:S(2)}, u32[]{:S(2)}) collective-permute-start(bf16[4,128,128]{2,1,0:T(8,128)(2,1)S(1)} %bitcast.250), channel_id=1, source_target_pairs={{0,6},{1,7},{2,8},{3,9},{4,10},{5,11},{6,12},{7,13},{8,14},{9,15},... | collective-permute-start | bytes 393224 | tf_op jit(solution)/shard_map/ppermute | solution.py:23
  51.0 40.5 %copy-start.2 = (bf16[1,256,2048]{2,1,0:T(8,128)(2,1)S(1)}, bf16[1,256,2048]{2,1,0:T(8,128)(2,1)}, u32[]{:S(2)}) copy-start(bf16[1,256,2048]{2,1,0:T(8,128)(2,1)} %param.10) | copy-start | bytes 3145732
  51.0 25.8 %collective-permute-start.5 = (bf16[4,128,128]{2,1,0:T(8,128)(2,1)}, bf16[4,128,128]{2,1,0:T(8,128)(2,1)S(1)}, u32[]{:S(2)}, u32[]{:S(2)}) collective-permute-start(bf16[4,128,128]{2,1,0:T(8,128)(2,1)} %bitcast.56), channel_id=1, source_target_pairs={{0,9},{1,10},{2,11},{3,12},{4,13},{5,14},{6,15},{7,0},{8,1},{9,2},... | collective-permute-start | bytes 393224 | tf_op jit(solution)/shard_map/ppermute | solution.py:23
  53.6 23.2 %collective-permute-start.6 = (bf16[4,128,128]{2,1,0:T(8,128)(2,1)S(1)}, bf16[4,128,128]{2,1,0:T(8,128)(2,1)S(1)}, u32[]{:S(2)}, u32[]{:S(2)}) collective-permute-start(bf16[4,128,128]{2,1,0:T(8,128)(2,1)S(1)} %bitcast.249), channel_id=1, source_target_pairs={{0,10},{1,11},{2,12},{3,13},{4,14},{5,15},{6,0},{7,1},{8,2},{9,3},... | collective-permute-start | bytes 393224 | tf_op jit(solution)/shard_map/ppermute | solution.py:23
  54.7 22.1 %collective-permute-start.4 = (bf16[4,128,128]{2,1,0:T(8,128)(2,1)}, bf16[4,128,128]{2,1,0:T(8,128)(2,1)S(1)}, u32[]{:S(2)}, u32[]{:S(2)}) collective-permute-start(bf16[4,128,128]{2,1,0:T(8,128)(2,1)} %bitcast.54), channel_id=1, source_target_pairs={{0,8},{1,9},{2,10},{3,11},{4,12},{5,13},{6,14},{7,15},{8,0},{9,1},... | collective-permute-start | bytes 393224 | tf_op jit(solution)/shard_map/ppermute | solution.py:23
  55.9 20.9 %collective-permute-start.3 = (bf16[4,128,128]{2,1,0:T(8,128)(2,1)}, bf16[4,128,128]{2,1,0:T(8,128)(2,1)S(1)}, u32[]{:S(2)}, u32[]{:S(2)}) collective-permute-start(bf16[4,128,128]{2,1,0:T(8,128)(2,1)} %bitcast.52), channel_id=1, source_target_pairs={{0,7},{1,8},{2,9},{3,10},{4,11},{5,12},{6,13},{7,14},{8,15},{9,0},... | collective-permute-start | bytes 393224 | tf_op jit(solution)/shard_map/ppermute | solution.py:23
  95.2 5.1 %copy-start.3 = (bf16[256,2048]{1,0:T(8,128)(2,1)S(1)}, bf16[256,2048]{1,0:T(8,128)(2,1)}, u32[]{:S(2)}) copy-start(bf16[256,2048]{1,0:T(8,128)(2,1)} %get-tuple-element.68) | copy-start | bytes 3145732
  95.8 7.8 %collective-permute-start.7 = (bf16[1,256,128]{1,2,0:T(8,128)(2,1)S(1)}, bf16[1,256,128]{1,2,0:T(8,128)(2,1)S(1)}, u32[]{:S(2)}, u32[]{:S(2)}) collective-permute-start(bf16[1,256,128]{1,2,0:T(8,128)(2,1)S(1)} %get-tuple-element.37), channel_id=1, source_target_pairs={{0,1},{1,2},{2,3},{3,4},{4,5},{5,6},{6,7},{7,8},{8,9},{9,10},{10,1... | collective-permute-start | bytes 196616 | tf_op jit(solution)/shard_map/ppermute | solution.py:14
  95.8 7.8 %collective-permute-start.8 = (bf16[1,256,128]{1,2,0:T(8,128)(2,1)S(1)}, bf16[1,256,128]{1,2,0:T(8,128)(2,1)S(1)}, u32[]{:S(2)}, u32[]{:S(2)}) collective-permute-start(bf16[1,256,128]{1,2,0:T(8,128)(2,1)S(1)} %get-tuple-element.39), channel_id=1, source_target_pairs={{1,0},{2,1},{3,2},{4,3},{5,4},{6,5},{7,6},{8,7},{9,8},{10,9},{11,1... | collective-permute-start | bytes 196616 | tf_op jit(solution)/shard_map/ppermute | solution.py:15
  100.3 5.3 %copy-start.10 = (pred[128]{0:T(512)(128)(4,1)S(1)}, pred[128]{0:T(512)(128)(4,1)}, u32[]{:S(2)}) copy-start(pred[128]{0:T(512)(128)(4,1)} %copy-done.9) | copy-start | bytes 388
  100.3 5.3 %copy-start.12 = (pred[128]{0:T(512)(128)(4,1)S(1)}, pred[128]{0:T(512)(128)(4,1)}, u32[]{:S(2)}) copy-start(pred[128]{0:T(512)(128)(4,1)} %copy-done.11) | copy-start | bytes 388
  128.9 2.0 %copy-start.4 = (bf16[256,2048]{1,0:T(8,128)(2,1)S(1)}, bf16[256,2048]{1,0:T(8,128)(2,1)}, u32[]{:S(2)}) copy-start(bf16[256,2048]{1,0:T(8,128)(2,1)} %get-tuple-element.68) | copy-start | bytes 3145732
  128.9 3.3 %copy-start.1 = (bf16[2,128,256]{2,1,0:T(8,128)(2,1)S(1)}, bf16[2,128,256]{2,1,0:T(8,128)(2,1)}, u32[]{:S(2)}) copy-start(bf16[2,128,256]{2,1,0:T(8,128)(2,1)} %param.13) | copy-start | bytes 393220
where the time goes:
time: 133 us; the launch traced here: 132 us
  matrix products  41.2 us (31%)
  other arithmetic  37.2 us (28%)
  waiting for transfers between devices  18.8 us (14%)
  local copies, waits for them, and re-layouts  17.3 us (13%)
  starting transfers between devices  17.1 us (13%)
    unnamed x18, matrix products  35.1 us
    ppermute x5, waiting for transfers between devices, passed_along(): return lax.ppermute(value, axis, pairs)  18.8 us
    scatter-add x1, other arithmetic, remap_add(): summed.at[target_table.reshape(-1)]  14.6 us
    add x2, other arithmetic, residual_block(): convolved + jnp.einsum('io,irc->orc', kernel[row_off * 3 + col_off], shif...  11.3 us
    ppermute x2, starting transfers between devices, with_halo(): after = lax.ppermute(first, axis, down)  9.46 us
    ppermute x5, starting transfers between devices, passed_along(): return lax.ppermute(value, axis, pairs)  7.11 us
    concatenate x4, other arithmetic, residual_block(): jnp.concatenate([lower_row[:, None], activated, upper_row[:, None]], axis=1)  6.48 us
    reshape x3, local copies, waits for them, and re-layouts, residual_block(): convolved.reshape(channels, cell_count)  5.7 us
  transfers between devices with their start and end apart: 9, of which 1 were waited for; matrix products, arithmetic and copies ran while one was open for 8% of the time, Pallas kernels for 0%

commit v1 on v0

v1 whole, which is shorter than its diff:
```python
import functools

import jax
import jax.numpy as jnp
from jax import lax
from jax.experimental import pallas as pl
from jax.experimental.pallas import tpu as pltpu
from jax.sharding import PartitionSpec as P

F32 = jnp.float32
BF16 = jnp.bfloat16


def gelu(x):
    return jax.nn.gelu(x, approximate=True)


def spread(row, width):
    return jnp.broadcast_to(row, (width, row.shape[1])).T


def forecast_kernel(
    tiles,
    features,
    conv_weight,
    proj_weight,
    back_weight,
    sea_fraction,
    halo_source,
    src_cells,
    dst_cells,
    out,
    xs,
    st,
    pad,
    cw,
    pw,
    bw,
    sea,
    halo,
    src,
    dst,
    wet,
    srcb,
    hot_low,
    hot_up,
    edge,
    proj,
    outgoing,
    incoming,
    land,
    summed,
    result,
    in_sem,
    out_dma_sem,
    halo_send,
    halo_recv,
    block_send,
    block_recv,
):
    half = tiles // 2
    me = lax.axis_index("tiles")
    pos = lax.rem(me + half // 2, tiles)
    comp = pos // half
    local = lax.rem(pos, half)
    channels, cells = xs.shape
    row = halo.shape[1]
    rows = cells // row
    offsets = incoming.shape[0]
    per_slot = incoming.shape[1]
    reach = offsets // 2
    coupling = pw.shape[1]
    up = lax.rem(me + 1, tiles)
    down = lax.rem(me + tiles - 1, tiles)

    def local_copy(source, target, slot):
        return pltpu.make_async_copy(source, target, in_sem.at[slot])

    loads = [
        local_copy(features.at[0], xs, 0),
        local_copy(halo_source.at[0], halo, 1),
        local_copy(src_cells, src, 2),
        local_copy(dst_cells, dst, 3),
        local_copy(sea_fraction, sea, 4),
        local_copy(conv_weight.at[comp, 0], cw.at[0], 5),
        local_copy(proj_weight.at[comp], pw, 6),
        local_copy(back_weight.at[comp], bw, 7),
        local_copy(conv_weight.at[comp, 1], cw.at[1], 8),
    ]
    for load in loads:
        load.start()

    def partner(slot):
        return lax.rem(me + half + slot - reach + tiles, tiles)

    barrier = pltpu.get_barrier_semaphore()
    for other in [up, down] + [partner(s) for s in range(offsets)]:
        pl.semaphore_signal(
            barrier, inc=1, device_id={"tiles": other}, device_id_type=pl.DeviceIdType.MESH
        )

    def at(r):
        return pl.ds(pl.multiple_of(r * row, row), row)

    def put_activated(r, x):
        g = gelu(x)
        where = at(r + 1)
        pad[where, 0:channels] = pltpu.roll(g, 1, 0).astype(BF16)
        pad[where, channels : 2 * channels] = g.astype(BF16)
        pad[where, 2 * channels : 3 * channels] = pltpu.roll(g, row - 1, 0).astype(BF16)

    def halo_copies(block):
        mid = pl.ds(channels, channels)
        to_down = pltpu.make_async_remote_copy(
            src_ref=pad.at[pl.ds(row, row), mid],
            dst_ref=edge.at[block, 1, pl.ds(0, row)],
            send_sem=halo_send.at[block, 0],
            recv_sem=halo_recv.at[block, 1],
            device_id={"tiles": down},
            device_id_type=pl.DeviceIdType.MESH,
        )
        to_up = pltpu.make_async_remote_copy(
            src_ref=pad.at[pl.ds(rows * row, row), mid],
            dst_ref=edge.at[block, 0, pl.ds(0, row)],
            send_sem=halo_send.at[block, 1],
            recv_sem=halo_recv.at[block, 0],
            device_id={"tiles": up},
            device_id_type=pl.DeviceIdType.MESH,
        )
        return to_down, to_up

    def conv(block, first, count):
        span = count * row
        windows = [
            pad[pl.ds(pl.multiple_of((first + a) * row, row), span), :] for a in range(3)
        ]
        taps = cw[block].reshape(9 * channels, channels)
        return jnp.dot(
            jnp.concatenate(windows, axis=1), taps, preferred_element_type=F32
        )

    def updated(block, first, count):
        where = pl.ds(pl.multiple_of(first * row, row), count * row)
        w = wet[where, :]
        w = jnp.concatenate([w] * (channels // w.shape[1]), axis=1)
        return (st[where, :].astype(F32) + w * conv(block, first, count)).astype(BF16)

    def place_halo(block):
        for side, hot, target in ((0, hot_low, 0), (1, hot_up, rows + 1)):
            own = pad[pl.ds(row if side == 0 else rows * row, row), channels : 2 * channels]
            pair = jnp.concatenate([edge[block, side], own], axis=0)
            taken = jnp.dot(hot[...], pair, preferred_element_type=F32).astype(BF16)
            for b in range(3):
                pad[pl.ds(target * row, row), b * channels : (b + 1) * channels] = taken[
                    b * row : (b + 1) * row
                ]

    def load_row(r):
        x = xs[:, at(r)].astype(F32).T
        st[at(r), :] = x.astype(BF16)
        put_activated(r, x)

    loads[0].wait()
    load_row(0)
    load_row(rows - 1)
    pl.semaphore_wait(barrier, offsets + 2)
    for copy in halo_copies(0):
        copy.start()

    @pl.loop(1, rows - 1)
    def _(r):
        load_row(r)

    for load in loads[1:5]:
        load.wait()

    for side, hot in ((0, hot_low), (1, hot_up)):
        column = spread(halo[side : side + 1, :], row)
        column = jnp.concatenate([column, column], axis=1)
        lane = lax.broadcasted_iota(jnp.int32, column.shape, 1)
        one = jnp.where(column == lane, 1.0, 0.0).astype(F32)
        hot[0:row] = pltpu.roll(one, 1, 0).astype(BF16)
        hot[row : 2 * row] = one.astype(BF16)
        hot[2 * row : 3 * row] = pltpu.roll(one, row - 1, 0).astype(BF16)

    for r in range(rows):
        values = spread(sea[0:1, r * row : (r + 1) * row], row)
        wet[r * row : (r + 1) * row, :] = jnp.where(comp == 1, values, F32(1.0))

    for s in range(offsets):
        for e in range(per_slot // row):
            index = s * (per_slot // row) + e
            srcb[index * row : (index + 1) * row, :] = spread(src[0, s, e : e + 1, :], row)

    loads[5].wait()
    loads[6].wait()

    def block_zero(first, count):
        new = updated(0, first, count)
        where = pl.ds(pl.multiple_of(first * row, row), count * row)
        st[where, :] = new
        proj[where, :] = jnp.dot(new, pw[...], preferred_element_type=F32).astype(BF16)

    group = (rows - 2) // 2

    @pl.loop(0, 2)
    def _(g):
        block_zero(1 + g * group, group)

    for copy in halo_copies(0):
        copy.wait()
    place_halo(0)
    block_zero(0, 1)
    block_zero(rows - 1, 1)

    def block_copy(s):
        return pltpu.make_async_remote_copy(
            src_ref=outgoing.at[s],
            dst_ref=incoming.at[s],
            send_sem=block_send.at[s],
            recv_sem=block_recv.at[s],
            device_id={"tiles": partner(s)},
            device_id_type=pl.DeviceIdType.MESH,
        )

    def sends(s):
        there = local + s - reach
        return jnp.logical_and(there >= 0, there < half)

    def receives(s):
        there = local - s + reach
        return jnp.logical_and(there >= 0, there < half)

    order = sorted(range(offsets), key=lambda s: (abs(s - reach), s))

    for s in order:
        @pl.when(sends(s))
        def _(s=s):
            lane = lax.broadcasted_iota(jnp.int32, (per_slot, row), 1)
            cell = srcb[s * per_slot : (s + 1) * per_slot, :]
            hot = jnp.concatenate(
                [jnp.where(cell == lane + r * row, 1.0, 0.0).astype(BF16) for r in range(rows)],
                axis=1,
            )
            outgoing[s] = jnp.dot(hot, proj[...], preferred_element_type=F32).astype(BF16)
            block_copy(s).start()

    @pl.loop(0, rows)
    def _(r):
        cell = lax.broadcasted_iota(jnp.int32, (row, row), 0) + r * row
        for s in range(offsets):
            for e in range(per_slot // row):
                target = dst[0, s, e : e + 1, :]
                land[at(r), s * per_slot + e * row : s * per_slot + (e + 1) * row] = jnp.where(
                    target == cell, 1.0, 0.0
                ).astype(BF16)

    summed[...] = jnp.zeros_like(summed)
    loads[7].wait()
    loads[8].wait()

    chunk = 4 * row
    for s in order:
        @pl.when(receives(s))
        def _(s=s):
            block_copy(s).wait_recv()

            @pl.loop(0, cells // chunk)
            def _(c):
                where = pl.ds(pl.multiple_of(c * chunk, chunk), chunk)
                summed[where, :] += jnp.dot(
                    land[where, s * per_slot : (s + 1) * per_slot],
                    incoming[s],
                    preferred_element_type=F32,
                )

    def add_back(r):
        remapped = summed[at(r), :].astype(BF16)
        returned = jnp.dot(remapped, bw[...], preferred_element_type=F32)
        new = (st[at(r), :].astype(F32) + returned).astype(BF16)
        st[at(r), :] = new
        put_activated(r, new.astype(F32))

    add_back(0)
    add_back(rows - 1)
    for copy in halo_copies(1):
        copy.start()

    @pl.loop(1, rows - 1)
    def _(r):
        add_back(r)

    def block_one(first, count):
        new = updated(1, first, count).astype(F32)
        for i in range(count):
            result[:, at(first + i)] = new[i * row : (i + 1) * row].T.astype(BF16)

    def result_copy(first, count, slot):
        lanes = pl.ds(first * row, count * row)
        return pltpu.make_async_copy(
            result.at[:, lanes], out.at[0, :, lanes], out_dma_sem.at[slot]
        )

    @pl.loop(0, 2)
    def _(g):
        block_one(1 + g * group, group)

    middle = result_copy(1, rows - 2, 0)
    middle.start()
    for copy in halo_copies(1):
        copy.wait()
    place_halo(1)
    block_one(0, 1)
    low = result_copy(0, 1, 1)
    low.start()
    block_one(rows - 1, 1)
    high = result_copy(rows - 1, 1, 2)
    high.start()
    for s in order:
        @pl.when(sends(s))
        def _(s=s):
            block_copy(s).wait_send()
    middle.wait()
    low.wait()
    high.wait()


def on_device(
    features, conv_weight, proj_weight, back_weight, sea_fraction, halo_source, src_cells, dst_cells
):
    tiles = lax.axis_size("tiles")
    _, channels, cells = features.shape
    row = halo_source.shape[2]
    _, offsets, slots, block = src_cells.shape
    coupling = proj_weight.shape[2]
    per_slot = slots * block
    rows = cells // row
    taps = conv_weight.shape[2]
    flops = 4 * cells * taps * channels * channels + 4 * offsets * per_slot * cells * coupling
    return pl.pallas_call(
        functools.partial(forecast_kernel, tiles),
        out_shape=jax.ShapeDtypeStruct(features.shape, BF16),
        in_specs=[pl.BlockSpec(memory_space=pl.ANY)] * 8,
        out_specs=pl.BlockSpec(memory_space=pl.ANY),
        scratch_shapes=[
            pltpu.VMEM((channels, cells), BF16),
            pltpu.VMEM((cells, channels), BF16),
            pltpu.VMEM(((rows + 2) * row, 3 * channels), BF16),
            pltpu.VMEM((2, taps, channels, channels), BF16),
            pltpu.VMEM((channels, coupling), BF16),
            pltpu.VMEM((coupling, channels), BF16),
            pltpu.VMEM((1, cells), F32),
            pltpu.VMEM((2, row), jnp.int32),
            pltpu.VMEM(src_cells.shape, jnp.int32),
            pltpu.VMEM(dst_cells.shape, jnp.int32),
            pltpu.VMEM((cells, row), F32),
            pltpu.VMEM((offsets * per_slot, row), jnp.int32),
            pltpu.VMEM((3 * row, 2 * row), BF16),
            pltpu.VMEM((3 * row, 2 * row), BF16),
            pltpu.VMEM((2, 2, row, channels), BF16),
            pltpu.VMEM((cells, coupling), BF16),
            pltpu.VMEM((offsets, per_slot, coupling), BF16),
            pltpu.VMEM((offsets, per_slot, coupling), BF16),
            pltpu.VMEM((cells, offsets * per_slot), BF16),
            pltpu.VMEM((cells, coupling), F32),
            pltpu.VMEM((channels, cells), BF16),
            pltpu.SemaphoreType.DMA((9,)),
            pltpu.SemaphoreType.DMA((3,)),
            pltpu.SemaphoreType.DMA((2, 2)),
            pltpu.SemaphoreType.DMA((2, 2)),
            pltpu.SemaphoreType.DMA((offsets,)),
            pltpu.SemaphoreType.DMA((offsets,)),
        ],
        compiler_params=pltpu.CompilerParams(
            collective_id=0, has_side_effects=True, vmem_limit_bytes=56 * 1024 * 1024
        ),
        cost_estimate=pl.CostEstimate(
            flops=flops, bytes_accessed=8 * channels * cells, transcendentals=2 * channels * cells
        ),
    )(
        features,
        conv_weight,
        proj_weight,
        back_weight,
        sea_fraction,
        halo_source,
        src_cells,
        dst_cells,
    )


def solution(mesh):
    placed = (
        P(("runs", "tiles"), None, None),
        P(),
        P(),
        P(),
        P("tiles", None),
        P("tiles", None, None),
        P("tiles", None, None, None),
        P("tiles", None, None, None),
    )
    return jax.shard_map(
        on_device,
        mesh=mesh,
        in_specs=placed,
        out_specs=P(("runs", "tiles"), None, None),
        check_vma=False,
    )
```

time: 133 us -> 47.2 us (0.35)
  Pallas kernels: 0 us -> 44.8 us
  matrix products: 41.2 us -> 0 us
  other arithmetic: 37.2 us -> 0 us
  waiting for transfers between devices: 18.8 us -> 0 us
  starting transfers between devices: 17.1 us -> 0 us
  local copies, waits for them, and re-layouts: 17.3 us -> 2.3 us
    pallas_call x0 -> x1, Pallas kernels: none -> 44.8 us  [on_device(): pl.pallas_call(functools.partial(forecast_kernel, tiles), out_shape=jax.S...]
    unnamed x18 -> x0, matrix products: 35.1 us -> none
    ppermute x9 -> x0, waiting for transfers between devices: 18.8 us -> none  [the longest x5 18.8 us: passed_along(): return lax.ppermute(value, axis, pairs)]
    ppermute x9 -> x0, starting transfers between devices: 17.1 us -> none  [the longest x2 9.46 us: with_halo(): after = lax.ppermute(first, axis, down)]
    scatter-add x1 -> x0, other arithmetic: 14.6 us -> none  [remap_add(): summed.at[target_table.reshape(-1)]]
    add x2 -> x0, other arithmetic: 11.3 us -> none  [residual_block(): convolved + jnp.einsum('io,irc->orc', kernel[row_off * 3 + col_off], shif...]
    gather x5 -> x0, local copies, waits for them, and re-layouts: 8.58 us -> none  [the longest x1 5.07 us: remap_add(): outgoing = projected[source_table]]
    concatenate x10 -> x0, other arithmetic: 7.72 us -> none  [the longest x4 6.48 us: residual_block(): jnp.concatenate([lower_row[:, None], activated, upper_row[:, None]], axis=1)]
  transfers between devices with their start and end apart: 9 -> 0, of which waited for: 1 -> 0; matrix products, arithmetic and copies ran while one was open for 8% -> 0% of each run, Pallas kernels for 0% -> 0%
where the time goes in v1:
time: 47.2 us; the launch traced here: 47.1 us
  Pallas kernels  44.8 us (95%)
  local copies, waits for them, and re-layouts  2.3 us (5%)
    pallas_call x1, Pallas kernels, on_device(): pl.pallas_call(functools.partial(forecast_kernel, tiles), out_shape=jax.S...  44.8 us
    unnamed x1, local copies, waits for them, and re-layouts  2.3 us

profile of v1, /device:TPU:0, one launch (start us, length us, event | category | flops | bytes accessed | tf_op | source)
XLA Modules:
  0.0 47.1 jit_solution(16650782303748872214)
XLA Ops:
  0.0 44.8 %shard_map.82 = bf16[1,256,2048]{2,1,0:T(8,128)(2,1)} custom-call(bf16[1,256,2048]{2,1,0:T(8,128)(2,1)} %features.1, bf16[2,2,9,256,256]{4,3,2,1,0:T(8,128)(2,1)} %conv_weight.1, bf16[2,256,128]{2,1,0:T(8,128)(2,1)} %proj_weight.1, bf16[2,128,256]{2,1,0:T(8,128)(2,1)} %back_weight.1, f32[1,2048]{1,0:T(1,128)} %sea_fraction.1, s32[1,2,128]{2,1,0:T(2,128)} %halo_source.1, ...), custom_call_target="tpu_custom_call" | custom-call | flops 7516192768 | bytes 4194304 | tf_op jit(solution)/shard_map/pallas_call | solution.py:340
  44.8 2.3 %copy.10 = bf16[1,256,2048]{2,1,0:T(8,128)(2,1)} copy(bf16[1,256,2048]{2,1,0:T(8,128)(2,1)} %shard_map.82) | data formatting | bytes 2097152

commit v2 on v1

--- a/solution.py
+++ b/solution.py
@@ -50,9 +50,7 @@
     incoming,
     land,
     summed,
-    result,
     in_sem,
-    out_dma_sem,
     halo_send,
     halo_recv,
     block_send,
@@ -77,13 +75,13 @@
         return pltpu.make_async_copy(source, target, in_sem.at[slot])
 
     loads = [
-        local_copy(features.at[0], xs, 0),
         local_copy(halo_source.at[0], halo, 1),
         local_copy(src_cells, src, 2),
-        local_copy(dst_cells, dst, 3),
         local_copy(sea_fraction, sea, 4),
+        local_copy(features.at[0], xs, 0),
         local_copy(conv_weight.at[comp, 0], cw.at[0], 5),
         local_copy(proj_weight.at[comp], pw, 6),
+        local_copy(dst_cells, dst, 3),
         local_copy(back_weight.at[comp], bw, 7),
         local_copy(conv_weight.at[comp, 1], cw.at[1], 8),
     ]
@@ -160,18 +158,7 @@
         st[at(r), :] = x.astype(BF16)
         put_activated(r, x)
 
-    loads[0].wait()
-    load_row(0)
-    load_row(rows - 1)
-    pl.semaphore_wait(barrier, offsets + 2)
-    for copy in halo_copies(0):
-        copy.start()
-
-    @pl.loop(1, rows - 1)
-    def _(r):
-        load_row(r)
-
-    for load in loads[1:5]:
+    for load in loads[0:3]:
         load.wait()
 
     for side, hot in ((0, hot_low), (1, hot_up)):
@@ -183,17 +170,34 @@
         hot[row : 2 * row] = one.astype(BF16)
         hot[2 * row : 3 * row] = pltpu.roll(one, row - 1, 0).astype(BF16)
 
-    for r in range(rows):
-        values = spread(sea[0:1, r * row : (r + 1) * row], row)
-        wet[r * row : (r + 1) * row, :] = jnp.where(comp == 1, values, F32(1.0))
-
-    for s in range(offsets):
-        for e in range(per_slot // row):
-            index = s * (per_slot // row) + e
-            srcb[index * row : (index + 1) * row, :] = spread(src[0, s, e : e + 1, :], row)
-
+    @pl.loop(0, rows)
+    def _(r):
+        values = spread(sea[0:1, at(r)], row)
+        wet[at(r), :] = jnp.where(comp == 1, values, F32(1.0))
+
+    slots = per_slot // row
+
+    @pl.loop(0, offsets)
+    def _(s):
+        for e in range(slots):
+            srcb[at(s * slots + e), :] = spread(src[0, s, e : e + 1, :], row)
+
+    loads[3].wait()
+
+    @pl.loop(0, 2)
+    def _(g):
+        load_row(g * (rows - 1))
+
+    pl.semaphore_wait(barrier, offsets + 2)
+    for copy in halo_copies(0):
+        copy.start()
+
+    @pl.loop(1, rows - 1)
+    def _(r):
+        load_row(r)
+
+    loads[4].wait()
     loads[5].wait()
-    loads[6].wait()
 
     def block_zero(first, count):
         new = updated(0, first, count)
@@ -201,17 +205,19 @@
         st[where, :] = new
         proj[where, :] = jnp.dot(new, pw[...], preferred_element_type=F32).astype(BF16)
 
-    group = (rows - 2) // 2
-
-    @pl.loop(0, 2)
+    group = 2
+
+    @pl.loop(0, (rows - 2) // group)
     def _(g):
         block_zero(1 + g * group, group)
 
     for copy in halo_copies(0):
         copy.wait()
     place_halo(0)
-    block_zero(0, 1)
-    block_zero(rows - 1, 1)
+
+    @pl.loop(0, 2)
+    def _(g):
+        block_zero(g * (rows - 1), 1)
 
     def block_copy(s):
         return pltpu.make_async_remote_copy(
@@ -231,13 +237,17 @@
         there = local - s + reach
         return jnp.logical_and(there >= 0, there < half)
 
-    order = sorted(range(offsets), key=lambda s: (abs(s - reach), s))
-
-    for s in order:
+    def slot_at(k):
+        return reach + (1 - 2 * lax.rem(k, 2)) * ((k + 1) // 2)
+
+    @pl.loop(0, offsets)
+    def _(k):
+        s = slot_at(k)
+
         @pl.when(sends(s))
-        def _(s=s):
+        def _():
             lane = lax.broadcasted_iota(jnp.int32, (per_slot, row), 1)
-            cell = srcb[s * per_slot : (s + 1) * per_slot, :]
+            cell = srcb[pl.ds(pl.multiple_of(s * per_slot, per_slot), per_slot), :]
             hot = jnp.concatenate(
                 [jnp.where(cell == lane + r * row, 1.0, 0.0).astype(BF16) for r in range(rows)],
                 axis=1,
@@ -245,11 +255,13 @@
             outgoing[s] = jnp.dot(hot, proj[...], preferred_element_type=F32).astype(BF16)
             block_copy(s).start()
 
+    loads[6].wait()
+
     @pl.loop(0, rows)
     def _(r):
         cell = lax.broadcasted_iota(jnp.int32, (row, row), 0) + r * row
         for s in range(offsets):
-            for e in range(per_slot // row):
+            for e in range(slots):
                 target = dst[0, s, e : e + 1, :]
                 land[at(r), s * per_slot + e * row : s * per_slot + (e + 1) * row] = jnp.where(
                     target == cell, 1.0, 0.0
@@ -260,16 +272,19 @@
     loads[8].wait()
 
     chunk = 4 * row
-    for s in order:
+    @pl.loop(0, offsets)
+    def _(k):
+        s = slot_at(k)
+
         @pl.when(receives(s))
-        def _(s=s):
+        def _():
             block_copy(s).wait_recv()
 
             @pl.loop(0, cells // chunk)
             def _(c):
                 where = pl.ds(pl.multiple_of(c * chunk, chunk), chunk)
                 summed[where, :] += jnp.dot(
-                    land[where, s * per_slot : (s + 1) * per_slot],
+                    land[where, pl.ds(pl.multiple_of(s * per_slot, per_slot), per_slot)],
                     incoming[s],
                     preferred_element_type=F32,
                 )
@@ -281,8 +296,10 @@
         st[at(r), :] = new
         put_activated(r, new.astype(F32))
 
-    add_back(0)
-    add_back(rows - 1)
+    @pl.loop(0, 2)
+    def _(g):
+        add_back(g * (rows - 1))
+
     for copy in halo_copies(1):
         copy.start()
 
@@ -293,36 +310,25 @@
     def block_one(first, count):
         new = updated(1, first, count).astype(F32)
         for i in range(count):
-            result[:, at(first + i)] = new[i * row : (i + 1) * row].T.astype(BF16)
-
-    def result_copy(first, count, slot):
-        lanes = pl.ds(first * row, count * row)
-        return pltpu.make_async_copy(
-            result.at[:, lanes], out.at[0, :, lanes], out_dma_sem.at[slot]
-        )
-
-    @pl.loop(0, 2)
+            out[0, :, at(first + i)] = new[i * row : (i + 1) * row].T.astype(BF16)
+
+    @pl.loop(0, (rows - 2) // group)
     def _(g):
         block_one(1 + g * group, group)
 
-    middle = result_copy(1, rows - 2, 0)
-    middle.start()
     for copy in halo_copies(1):
         copy.wait()
     place_halo(1)
-    block_one(0, 1)
-    low = result_copy(0, 1, 1)
-    low.start()
-    block_one(rows - 1, 1)
-    high = result_copy(rows - 1, 1, 2)
-    high.start()
-    for s in order:
+
+    @pl.loop(0, 2)
+    def _(g):
+        block_one(g * (rows - 1), 1)
+
+    @pl.loop(0, offsets)
+    def _(s):
         @pl.when(sends(s))
-        def _(s=s):
+        def _():
             block_copy(s).wait_send()
-    middle.wait()
-    low.wait()
-    high.wait()
 
 
 def on_device(
@@ -340,8 +346,8 @@
     return pl.pallas_call(
         functools.partial(forecast_kernel, tiles),
         out_shape=jax.ShapeDtypeStruct(features.shape, BF16),
-        in_specs=[pl.BlockSpec(memory_space=pl.ANY)] * 8,
-        out_specs=pl.BlockSpec(memory_space=pl.ANY),
+        in_specs=[pl.BlockSpec(memory_space=pltpu.HBM)] * 8,
+        out_specs=pl.BlockSpec(memory_space=pltpu.VMEM),
         scratch_shapes=[
             pltpu.VMEM((channels, cells), BF16),
             pltpu.VMEM((cells, channels), BF16),
@@ -363,29 +369,32 @@
             pltpu.VMEM((offsets, per_slot, coupling), BF16),
             pltpu.VMEM((cells, offsets * per_slot), BF16),
             pltpu.VMEM((cells, coupling), F32),
-            pltpu.VMEM((channels, cells), BF16),
             pltpu.SemaphoreType.DMA((9,)),
-            pltpu.SemaphoreType.DMA((3,)),
             pltpu.SemaphoreType.DMA((2, 2)),
             pltpu.SemaphoreType.DMA((2, 2)),
             pltpu.SemaphoreType.DMA((offsets,)),
             pltpu.SemaphoreType.DMA((offsets,)),
         ],
         compiler_params=pltpu.CompilerParams(
-            collective_id=0, has_side_effects=True, vmem_limit_bytes=56 * 1024 * 1024
+            collective_id=0, has_side_effects=True, vmem_limit_bytes=40 * 1024 * 1024
         ),
         cost_estimate=pl.CostEstimate(
             flops=flops, bytes_accessed=8 * channels * cells, transcendentals=2 * channels * cells
         ),
     )(
-        features,
-        conv_weight,
-        proj_weight,
-        back_weight,
-        sea_fraction,
-        halo_source,
-        src_cells,
-        dst_cells,
+        *(
+            pltpu.with_memory_space_constraint(value, pltpu.HBM)
+            for value in (
+                features,
+                conv_weight,
+                proj_weight,
+                back_weight,
+                sea_fraction,
+                halo_source,
+                src_cells,
+                dst_cells,
+            )
+        )
     )
 
 

time: 47.2 us -> 49.5 us (1.049)
  Pallas kernels: 44.8 us -> 48.4 us
  local copies, waits for them, and re-layouts: 2.3 us -> 0.97 us
    pallas_call x1, Pallas kernels: 44.8 us -> 48.4 us  [on_device(): pl.pallas_call(functools.partial(forecast_kernel, tiles), out_shape=jax.S...]
    unnamed x1, local copies, waits for them, and re-layouts: 2.3 us -> 0.97 us
where the time goes in v2:
time: 49.5 us; the launch traced here: 49.3 us
  Pallas kernels  48.4 us (98%)
  local copies, waits for them, and re-layouts  0.97 us (2%)
    pallas_call x1, Pallas kernels, on_device(): pl.pallas_call(functools.partial(forecast_kernel, tiles), out_shape=jax.S...  48.4 us

profile of v2, /device:TPU:0, one launch (start us, length us, event | category | flops | bytes accessed | tf_op | source)
XLA Modules:
  0.0 49.3 jit_solution(11146587064587840998)
XLA Ops:
  0.0 48.4 %shard_map.82 = bf16[1,256,2048]{2,1,0:T(8,128)(2,1)S(1)} custom-call(bf16[1,256,2048]{2,1,0:T(8,128)(2,1)} %features.1, bf16[2,2,9,256,256]{4,3,2,1,0:T(8,128)(2,1)} %conv_weight.1, bf16[2,256,128]{2,1,0:T(8,128)(2,1)} %proj_weight.1, bf16[2,128,256]{2,1,0:T(8,128)(2,1)} %back_weight.1, f32[1,2048]{1,0:T(1,128)} %sea_fraction.1, s32[1,2,128]{2,1,0:T(2,128)} %halo_source.1, ...), custom_call_target="tpu_custom_call" | custom-call | flops 7516192768 | bytes 4194304 | tf_op jit(solution)/shard_map/pallas_call | solution.py:346
  48.4 1.0 %copy.10 = bf16[1,256,2048]{2,1,0:T(8,128)(2,1)} copy(bf16[1,256,2048]{2,1,0:T(8,128)(2,1)S(1)} %shard_map.82) | data formatting | bytes 2097152

commit v3 on v2

--- a/solution.py
+++ b/solution.py
@@ -127,21 +127,31 @@
         )
         return to_down, to_up
 
-    def conv(block, first, count):
-        span = count * row
+    def conv(block, pieces):
         windows = [
-            pad[pl.ds(pl.multiple_of((first + a) * row, row), span), :] for a in range(3)
+            jnp.concatenate(
+                [pad[first * row + a * row : (first + count + a) * row, :] for a in range(3)],
+                axis=1,
+            )
+            for first, count in pieces
         ]
         taps = cw[block].reshape(9 * channels, channels)
         return jnp.dot(
-            jnp.concatenate(windows, axis=1), taps, preferred_element_type=F32
-        )
-
-    def updated(block, first, count):
-        where = pl.ds(pl.multiple_of(first * row, row), count * row)
-        w = wet[where, :]
+            jnp.concatenate(windows, axis=0), taps, preferred_element_type=F32
+        )
+
+    def span(ref, pieces):
+        return jnp.concatenate(
+            [ref[first * row : (first + count) * row, :] for first, count in pieces], axis=0
+        )
+
+    def updated(block, pieces):
+        w = span(wet, pieces)
         w = jnp.concatenate([w] * (channels // w.shape[1]), axis=1)
-        return (st[where, :].astype(F32) + w * conv(block, first, count)).astype(BF16)
+        return (span(st, pieces).astype(F32) + w * conv(block, pieces)).astype(BF16)
+
+    inner = [(1, rows - 2)]
+    rim = [(0, 1), (rows - 1, 1)]
 
     def place_halo(block):
         for side, hot, target in ((0, hot_low, 0), (1, hot_up, rows + 1)):
@@ -170,54 +180,47 @@
         hot[row : 2 * row] = one.astype(BF16)
         hot[2 * row : 3 * row] = pltpu.roll(one, row - 1, 0).astype(BF16)
 
-    @pl.loop(0, rows)
-    def _(r):
-        values = spread(sea[0:1, at(r)], row)
-        wet[at(r), :] = jnp.where(comp == 1, values, F32(1.0))
+    for r in range(rows):
+        values = spread(sea[0:1, r * row : (r + 1) * row], row)
+        wet[r * row : (r + 1) * row, :] = jnp.where(comp == 1, values, F32(1.0))
 
     slots = per_slot // row
 
-    @pl.loop(0, offsets)
-    def _(s):
+    for s in range(offsets):
         for e in range(slots):
-            srcb[at(s * slots + e), :] = spread(src[0, s, e : e + 1, :], row)
+            i = s * slots + e
+            srcb[i * row : (i + 1) * row, :] = spread(src[0, s, e : e + 1, :], row)
 
     loads[3].wait()
 
-    @pl.loop(0, 2)
+    @pl.loop(0, rows // 2)
     def _(g):
-        load_row(g * (rows - 1))
+        load_row(2 * g)
+        load_row(2 * g + 1)
 
     pl.semaphore_wait(barrier, offsets + 2)
     for copy in halo_copies(0):
         copy.start()
 
-    @pl.loop(1, rows - 1)
-    def _(r):
-        load_row(r)
-
     loads[4].wait()
     loads[5].wait()
 
-    def block_zero(first, count):
-        new = updated(0, first, count)
-        where = pl.ds(pl.multiple_of(first * row, row), count * row)
-        st[where, :] = new
-        proj[where, :] = jnp.dot(new, pw[...], preferred_element_type=F32).astype(BF16)
-
-    group = 2
-
-    @pl.loop(0, (rows - 2) // group)
-    def _(g):
-        block_zero(1 + g * group, group)
-
+    def block_zero(pieces):
+        new = updated(0, pieces)
+        sent = jnp.dot(new, pw[...], preferred_element_type=F32).astype(BF16)
+        done = 0
+        for first, count in pieces:
+            where = slice(first * row, (first + count) * row)
+            part = slice(done * row, (done + count) * row)
+            st[where, :] = new[part]
+            proj[where, :] = sent[part]
+            done += count
+
+    block_zero(inner)
     for copy in halo_copies(0):
         copy.wait()
     place_halo(0)
-
-    @pl.loop(0, 2)
-    def _(g):
-        block_zero(g * (rows - 1), 1)
+    block_zero(rim)
 
     def block_copy(s):
         return pltpu.make_async_remote_copy(
@@ -271,7 +274,7 @@
     loads[7].wait()
     loads[8].wait()
 
-    chunk = 4 * row
+    chunk = 8 * row
     @pl.loop(0, offsets)
     def _(k):
         s = slot_at(k)
@@ -289,40 +292,41 @@
                     preferred_element_type=F32,
                 )
 
-    def add_back(r):
-        remapped = summed[at(r), :].astype(BF16)
+    def add_back(first, count):
+        where = pl.ds(pl.multiple_of(first * row, row), count * row)
+        remapped = summed[where, :].astype(BF16)
         returned = jnp.dot(remapped, bw[...], preferred_element_type=F32)
-        new = (st[at(r), :].astype(F32) + returned).astype(BF16)
-        st[at(r), :] = new
-        put_activated(r, new.astype(F32))
+        new = (st[where, :].astype(F32) + returned).astype(BF16)
+        st[where, :] = new
+        for i in range(count):
+            put_activated(first + i, new[i * row : (i + 1) * row].astype(F32))
 
     @pl.loop(0, 2)
     def _(g):
-        add_back(g * (rows - 1))
+        add_back(g * (rows - 1), 1)
 
     for copy in halo_copies(1):
         copy.start()
 
-    @pl.loop(1, rows - 1)
-    def _(r):
-        add_back(r)
-
-    def block_one(first, count):
-        new = updated(1, first, count).astype(F32)
-        for i in range(count):
-            out[0, :, at(first + i)] = new[i * row : (i + 1) * row].T.astype(BF16)
-
-    @pl.loop(0, (rows - 2) // group)
+    @pl.loop(0, 2)
     def _(g):
-        block_one(1 + g * group, group)
-
+        add_back(1 + g * ((rows - 2) // 2), (rows - 2) // 2)
+
+    def block_one(pieces):
+        new = updated(1, pieces).astype(F32)
+        done = 0
+        for first, count in pieces:
+            for i in range(first, first + count):
+                out[0, :, i * row : (i + 1) * row] = (
+                    new[done * row : (done + 1) * row].T.astype(BF16)
+                )
+                done += 1
+
+    block_one(inner)
     for copy in halo_copies(1):
         copy.wait()
     place_halo(1)
-
-    @pl.loop(0, 2)
-    def _(g):
-        block_one(g * (rows - 1), 1)
+    block_one(rim)
 
     @pl.loop(0, offsets)
     def _(s):

time: 49.5 us -> 43.1 us (0.87)
  Pallas kernels: 48.4 us -> 42 us
    pallas_call x1, Pallas kernels: 48.4 us -> 42 us  [on_device(): pl.pallas_call(functools.partial(forecast_kernel, tiles), out_shape=jax.S...]
where the time goes in v3:
time: 43.1 us; the launch traced here: 43 us
  Pallas kernels  42 us (97%)
  local copies, waits for them, and re-layouts  0.97 us (2%)
    pallas_call x1, Pallas kernels, on_device(): pl.pallas_call(functools.partial(forecast_kernel, tiles), out_shape=jax.S...  42 us
    unnamed x1, local copies, waits for them, and re-layouts  0.97 us

profile of v3, /device:TPU:0, one launch (start us, length us, event | category | flops | bytes accessed | tf_op | source)
XLA Modules:
  0.0 43.0 jit_solution(13026952747809945473)
XLA Ops:
  0.0 42.0 %shard_map.82 = bf16[1,256,2048]{2,1,0:T(8,128)(2,1)S(1)} custom-call(bf16[1,256,2048]{2,1,0:T(8,128)(2,1)} %features.1, bf16[2,2,9,256,256]{4,3,2,1,0:T(8,128)(2,1)} %conv_weight.1, bf16[2,256,128]{2,1,0:T(8,128)(2,1)} %proj_weight.1, bf16[2,128,256]{2,1,0:T(8,128)(2,1)} %back_weight.1, f32[1,2048]{1,0:T(1,128)} %sea_fraction.1, s32[1,2,128]{2,1,0:T(2,128)} %halo_source.1, ...), custom_call_target="tpu_custom_call" | custom-call | flops 7516192768 | bytes 4194304 | tf_op jit(solution)/shard_map/pallas_call | solution.py:350
  42.0 1.0 %copy.10 = bf16[1,256,2048]{2,1,0:T(8,128)(2,1)} copy(bf16[1,256,2048]{2,1,0:T(8,128)(2,1)S(1)} %shard_map.82) | data formatting | bytes 2097152

commit v4 on v3

--- a/solution.py
+++ b/solution.py
@@ -51,6 +51,7 @@
     land,
     summed,
     in_sem,
+    feature_sem,
     halo_send,
     halo_recv,
     block_send,
@@ -78,14 +79,26 @@
         local_copy(halo_source.at[0], halo, 1),
         local_copy(src_cells, src, 2),
         local_copy(sea_fraction, sea, 4),
-        local_copy(features.at[0], xs, 0),
         local_copy(conv_weight.at[comp, 0], cw.at[0], 5),
         local_copy(proj_weight.at[comp], pw, 6),
         local_copy(dst_cells, dst, 3),
         local_copy(back_weight.at[comp], bw, 7),
         local_copy(conv_weight.at[comp, 1], cw.at[1], 8),
     ]
-    for load in loads:
+    pieces_in = 4
+    quarter = rows // pieces_in
+
+    def piece_load(g):
+        lanes = pl.ds(pl.multiple_of(g * quarter * row, quarter * row), quarter * row)
+        return pltpu.make_async_copy(
+            features.at[0, :, lanes], xs.at[:, lanes], feature_sem.at[g]
+        )
+
+    for load in loads[:3]:
+        load.start()
+    for g in range(pieces_in):
+        piece_load(g).start()
+    for load in loads[3:]:
         load.start()
 
     def partner(slot):
@@ -191,19 +204,18 @@
             i = s * slots + e
             srcb[i * row : (i + 1) * row, :] = spread(src[0, s, e : e + 1, :], row)
 
-    loads[3].wait()
-
-    @pl.loop(0, rows // 2)
+    @pl.loop(0, pieces_in)
     def _(g):
-        load_row(2 * g)
-        load_row(2 * g + 1)
+        piece_load(g).wait()
+        for i in range(quarter):
+            load_row(quarter * g + i)
 
     pl.semaphore_wait(barrier, offsets + 2)
     for copy in halo_copies(0):
         copy.start()
 
+    loads[3].wait()
     loads[4].wait()
-    loads[5].wait()
 
     def block_zero(pieces):
         new = updated(0, pieces)
@@ -243,6 +255,24 @@
     def slot_at(k):
         return reach + (1 - 2 * lax.rem(k, 2)) * ((k + 1) // 2)
 
+    loads[5].wait()
+
+    def land_slot(s):
+        @pl.loop(0, rows // 4)
+        def _(q):
+            for i in range(4):
+                r = 4 * q + i
+                cell = lax.broadcasted_iota(jnp.int32, (row, row), 0) + r * row
+                hot = [
+                    jnp.where(dst[0, s, e : e + 1, :] == cell, 1.0, 0.0).astype(BF16)
+                    for e in range(slots)
+                ]
+                land[at(r), pl.ds(pl.multiple_of(s * per_slot, per_slot), per_slot)] = (
+                    jnp.concatenate(hot, axis=1)
+                )
+
+    in_flight = 2
+
     @pl.loop(0, offsets)
     def _(k):
         s = slot_at(k)
@@ -256,23 +286,22 @@
                 axis=1,
             )
             outgoing[s] = jnp.dot(hot, proj[...], preferred_element_type=F32).astype(BF16)
+
+        before = slot_at(lax.max(k - in_flight, 0))
+
+        @pl.when(jnp.logical_and(k >= in_flight, sends(before)))
+        def _():
+            block_copy(before).wait_send()
+
+        @pl.when(sends(s))
+        def _():
             block_copy(s).start()
 
+        land_slot(s)
+
+    summed[...] = jnp.zeros_like(summed)
     loads[6].wait()
-
-    @pl.loop(0, rows)
-    def _(r):
-        cell = lax.broadcasted_iota(jnp.int32, (row, row), 0) + r * row
-        for s in range(offsets):
-            for e in range(slots):
-                target = dst[0, s, e : e + 1, :]
-                land[at(r), s * per_slot + e * row : s * per_slot + (e + 1) * row] = jnp.where(
-                    target == cell, 1.0, 0.0
-                ).astype(BF16)
-
-    summed[...] = jnp.zeros_like(summed)
     loads[7].wait()
-    loads[8].wait()
 
     chunk = 8 * row
     @pl.loop(0, offsets)
@@ -328,8 +357,10 @@
     place_halo(1)
     block_one(rim)
 
-    @pl.loop(0, offsets)
-    def _(s):
+    @pl.loop(offsets - in_flight, offsets)
+    def _(k):
+        s = slot_at(k)
+
         @pl.when(sends(s))
         def _():
             block_copy(s).wait_send()
@@ -374,6 +405,7 @@
             pltpu.VMEM((cells, offsets * per_slot), BF16),
             pltpu.VMEM((cells, coupling), F32),
             pltpu.SemaphoreType.DMA((9,)),
+            pltpu.SemaphoreType.DMA((4,)),
             pltpu.SemaphoreType.DMA((2, 2)),
             pltpu.SemaphoreType.DMA((2, 2)),
             pltpu.SemaphoreType.DMA((offsets,)),

time: 43.1 us -> 45.9 us (1.065)
  Pallas kernels: 42 us -> 44.7 us
    pallas_call x1, Pallas kernels: 42 us -> 44.7 us  [on_device(): pl.pallas_call(functools.partial(forecast_kernel, tiles), out_shape=jax.S...]
where the time goes in v4:
time: 45.9 us; the launch traced here: 45.7 us
  Pallas kernels  44.7 us (97%)
  local copies, waits for them, and re-layouts  0.97 us (2%)
    pallas_call x1, Pallas kernels, on_device(): pl.pallas_call(functools.partial(forecast_kernel, tiles), out_shape=jax.S...  44.7 us
    unnamed x1, local copies, waits for them, and re-layouts  0.97 us

profile of v4, /device:TPU:0, one launch (start us, length us, event | category | flops | bytes accessed | tf_op | source)
XLA Modules:
  0.0 45.7 jit_solution(12197191282259510132)
XLA Ops:
  0.0 44.7 %shard_map.82 = bf16[1,256,2048]{2,1,0:T(8,128)(2,1)S(1)} custom-call(bf16[1,256,2048]{2,1,0:T(8,128)(2,1)} %features.1, bf16[2,2,9,256,256]{4,3,2,1,0:T(8,128)(2,1)} %conv_weight.1, bf16[2,256,128]{2,1,0:T(8,128)(2,1)} %proj_weight.1, bf16[2,128,256]{2,1,0:T(8,128)(2,1)} %back_weight.1, f32[1,2048]{1,0:T(1,128)} %sea_fraction.1, s32[1,2,128]{2,1,0:T(2,128)} %halo_source.1, ...), custom_call_target="tpu_custom_call" | custom-call | flops 7516192768 | bytes 4194304 | tf_op jit(solution)/shard_map/pallas_call | solution.py:381
  44.7 1.0 %copy.10 = bf16[1,256,2048]{2,1,0:T(8,128)(2,1)} copy(bf16[1,256,2048]{2,1,0:T(8,128)(2,1)S(1)} %shard_map.82) | data formatting | bytes 2097152
